TPU v7x, 32 devices: a whole 2x2x4 slice. The times are simulated.
32 devices in a mesh: tile: 16 (over z, y, x), rhs: 2 (over core).
Axes of the slice: x: 2, y: 2, z: 4, core: 2. Of those that a mesh axis runs over, the one named last changes fastest.
Arguments:
- sensitivity: bfloat16 [16384, 5120], P('tile', 'rhs'), may hold values from -0.0625 to 0.0625
- precision: float32 [5120], P('rhs'), may hold values from 3 to 60
- reaction: float32 [128, 128], P('tile'), may hold values from 0.25 to 2
- load: float32 [64, 16384], P(None, 'tile'), may hold values from -24 to 24
Outputs:
- solution: float32 [64, 16384], P(None, 'tile')
- residual: float32 [64, 16384], P(None, 'tile')
All inputs are finite; a program needn't handle non-finite values.
Results may differ from a plain program's by a relative error of at most 0.0042.
Values may be sent and summed in bfloat16 or wider, within the bound.
A program may use at most 64 MiB of HBM per device.

v0:
```python
import jax
import jax.numpy as jnp
from jax import lax
from jax.sharding import PartitionSpec as P

ITERS = 2


def with_halo(block, sides, width):
    for axis, dim in sides:
        count = lax.axis_size(axis)
        forward = [(i, i + 1) for i in range(count - 1)]
        backward = [(target, source) for source, target in forward]
        low = lax.ppermute(
            lax.slice_in_dim(block, block.shape[dim] - width, None, axis=dim), axis, forward
        )
        high = lax.ppermute(lax.slice_in_dim(block, 0, width, axis=dim), axis, backward)
        block = jnp.concatenate([low, block, high], axis=dim)
    return block


def stencil_rows(padded_field, reaction):
    sided = jnp.pad(padded_field, ((0, 0), (0, 0), (1, 1)))
    center = padded_field[:, 1:-1, :]
    neighbours = (
        padded_field[:, 2:, :] + padded_field[:, :-2, :] + sided[:, 1:-1, 2:] + sided[:, 1:-1, :-2]
    )
    return (reaction + 4.0) * center - neighbours


def single_rim(field, reaction):
    widened = with_halo(field, (("tile", 1),), 1)
    return stencil_rows(widened, reaction)


def joint_products(direction, residual, image):
    return lax.psum(
        (
            jnp.sum(residual * residual, axis=1),
            jnp.sum(direction * image, axis=1),
            jnp.sum(residual * image, axis=1),
            jnp.sum(image * image, axis=1),
        ),
        "tile",
    )


def per_device(sensitivity, precision, reaction, load):
    count_rhs = load.shape[0]
    strip_rows = reaction.shape[0]
    columns = reaction.shape[1]
    strip_index = lax.axis_index("tile")
    solution = jnp.zeros_like(load)
    residual = load
    direction = load
    current = None
    for iteration in range(ITERS):
        grid = direction.reshape(count_rhs, strip_rows, columns)
        twice = single_rim(single_rim(grid, reaction), reaction)
        lowered = direction.astype(jnp.bfloat16)
        partial_obs = jnp.dot(lowered, sensitivity, preferred_element_type=jnp.float32)
        owned = lax.psum_scatter(partial_obs, "tile", scatter_dimension=1, tiled=True)
        width = owned.shape[1]
        share = lax.dynamic_slice_in_dim(precision, strip_index * width, width)
        weighted = (share[None, :] * owned).astype(jnp.bfloat16)
        back_half = lax.dot_general(
            lax.all_gather(weighted, "tile", axis=1, tiled=True),
            sensitivity,
            (((1,), (1,)), ((), ())),
            preferred_element_type=jnp.float32,
        )
        image = lax.psum(back_half, "rhs") + twice.reshape(direction.shape)
        squared, curved, cross, image_sq = joint_products(direction, residual, image)
        if iteration == 0:
            current = squared
        alpha = current / curved
        solution = solution + alpha[:, None] * direction
        residual = residual - alpha[:, None] * image
        if iteration + 1 < ITERS:
            fresh = current - 2.0 * alpha * cross + alpha * alpha * image_sq
            direction = residual + (fresh / current)[:, None] * direction
            current = fresh
    return (solution, residual)


def solution(mesh):
    placed = (P("tile", "rhs"), P("rhs"), P("tile", None), P(None, "tile"))
    return jax.shard_map(
        per_device,
        mesh=mesh,
        in_specs=placed,
        out_specs=(P(None, "tile"), P(None, "tile")),
        check_vma=False,
    )
```

profile of v0, /device:TPU:0, one launch (start us, length us, event | category | flops | bytes accessed | tf_op | source)
XLA Modules:
  0.0 392.9 jit_solution(3618538398225299243)
XLA Ops:
  7.2 5.8 %convolution_bitcast_fusion.1 = f32[2560,64]{1,0:T(8,128)} fusion(bf16[1024,2560]{1,0:T(8,128)(2,1)} %param.4, f32[64,1024]{1,0:T(8,128)} %param.7), kind=kOutput, calls=%fused_computation.1 | convolution fusion | flops 335609856 | bytes 6160384
  13.3 4.8 %collective-permute-start.1 = (f32[64,1,128]{2,1,0:T(1,128)S(1)}, f32[64,1,128]{2,1,0:T(1,128)S(1)}, u32[]{:S(2)}, u32[]{:S(2)}) collective-permute-start(f32[64,1,128]{2,1,0:T(1,128)S(1)} %get-tuple-element.20), channel_id=1, source_target_pairs={{0,2},{2,4},{4,6},{6,8},{8,10},{10,12},{12,14},{14,16},{16,18},{18... | collective-permute-start | bytes 98312 | tf_op jit(solution)/shard_map/ppermute | solution.py:14
  18.1 1.3 collective-permute-start
  19.4 0.8 dynamic_slice.4
  20.2 3.7 collective-permute-done
  24.8 4.6 %collective-permute-start.3 = (f32[64,1,128]{2,1,0:T(1,128)S(1)}, f32[64,1,128]{2,1,0:T(1,128)S(1)}, u32[]{:S(2)}, u32[]{:S(2)}) collective-permute-start(f32[64,1,128]{2,1,0:T(1,128)S(1)} %get-tuple-element.18), channel_id=1, source_target_pairs={{0,2},{2,4},{4,6},{6,8},{8,10},{10,12},{12,14},{14,16},{16,18},{18... | collective-permute-start | bytes 98312 | tf_op jit(solution)/shard_map/ppermute | solution.py:14
  29.4 1.3 collective-permute-start.2
  30.7 64.1 %reduce-scatter.7.cloned.1.call-done = f32[160,64]{1,0:T(8,128)} async-done(((f32[2560,64]{1,0:T(8,128)}), f32[160,64]{1,0:T(8,128)}) %reduce-scatter.7.cloned.1.call-update) | async-done | bytes 40976
  94.8 1.0 copy.11
  95.7 39.1 %all-gather = bf16[16,160,64]{1,2,0:T(8,128)(2,1)S(1)} all-gather(bf16[1,160,64]{1,2,0:T(8,128)(2,1)S(1)} %fusion.11), channel_id=1, replica_groups=mesh['tile'=16,'rhs'=2] {'tile'}, dimensions={0}, use_global_device_ids=true | all-gather | bytes 348160 | tf_op jit(solution)/shard_map/all_gather | solution.py:67
  135.1 0.7 reshape.26
  135.9 4.9 %fusion.18 = f32[64,1024]{1,0:T(8,128)} fusion(bf16[2560,64]{0,1:T(8,128)(2,1)S(1)} %reshape.26, bf16[1024,2560]{1,0:T(8,128)(2,1)} %param.4), kind=kOutput, calls=%fused_computation.60 | convolution fusion | flops 335544320 | bytes 5832704 | tf_op jit(solution)/shard_map/dot_general | solution.py:66
  140.8 0.6 select_maximum_fusion.4
  141.7 14.5 %all-reduce.8.cloned.1.call-done = f32[64,1024]{1,0:T(8,128)} async-done(((f32[64,1024]{1,0:T(8,128)}), f32[64,1024]{1,0:T(8,128)}) %all-reduce.8.cloned.1.call-update) | async-done | bytes 262160 | tf_op jit(solution)/shard_map/psum | solution.py:72
  156.1 1.2 multiply_reduce_fusion.2
  157.3 42.0 %all-reduce.4 = (f32[64]{0:T(128)S(1)}, f32[64]{0:T(128)S(1)}, f32[64]{0:T(128)S(1)}) all-reduce(f32[64]{0:T(128)S(1)} %get-tuple-element.3, f32[64]{0:T(128)S(1)} %get-tuple-element.4, f32[64]{0:T(128)S(1)} %get-tuple-element.2), channel_id=1, replica_groups=mesh['tile'=16,'rhs'=2] {'tile'}, use_global_device_ids=true, to_apply=%region_7.8 | all-reduce | flops 192 | bytes 1536 | tf_op jit(solution)/shard_map/psum | solution.py:37
  199.4 5.7 %convolution_bitcast_fusion = f32[2560,64]{1,0:T(8,128)} fusion(bf16[1024,2560]{1,0:T(8,128)(2,1)} %param.4, f32[64,1024]{1,0:T(8,128)S(1)} %multiply_add_fusion.1), kind=kOutput, calls=%fused_computation | convolution fusion | flops 335609856 | bytes 6160384
  205.3 1.3 collective-permute-start.5
  206.6 1.3 collective-permute-start.4
  208.4 4.4 %collective-permute-done.4 = f32[64,1,128]{2,1,0:T(1,128)S(1)} collective-permute-done((f32[64,1,128]{2,1,0:T(1,128)S(1)}, f32[64,1,128]{2,1,0:T(1,128)S(1)}, u32[]{:S(2)}, u32[]{:S(2)}) %collective-permute-start.4) | collective-permute-done | bytes 32800 | tf_op jit(solution)/shard_map/ppermute | solution.py:17
  213.7 2.5 collective-permute-start.7
  216.2 1.3 collective-permute-start.6
  217.5 62.3 %reduce-scatter.9.cloned.1.call-done = f32[160,64]{1,0:T(8,128)} async-done(((f32[2560,64]{1,0:T(8,128)}), f32[160,64]{1,0:T(8,128)}) %reduce-scatter.9.cloned.1.call-update) | async-done | bytes 40976
  279.8 1.0 copy.13
  280.8 39.6 %all-gather.1 = bf16[16,160,64]{1,2,0:T(8,128)(2,1)S(1)} all-gather(bf16[1,160,64]{1,2,0:T(8,128)(2,1)S(1)} %fusion.12), channel_id=1, replica_groups=mesh['tile'=16,'rhs'=2] {'tile'}, dimensions={0}, use_global_device_ids=true | all-gather | bytes 348160 | tf_op jit(solution)/shard_map/all_gather | solution.py:67
  320.7 0.7 reshape.28
  321.4 4.9 %fusion.19 = f32[64,1024]{1,0:T(8,128)} fusion(bf16[2560,64]{0,1:T(8,128)(2,1)S(1)} %reshape.28, bf16[1024,2560]{1,0:T(8,128)(2,1)} %param.4), kind=kOutput, calls=%fused_computation.61 | convolution fusion | flops 335544320 | bytes 5832704 | tf_op jit(solution)/shard_map/dot_general | solution.py:66
  326.3 0.6 select_maximum_fusion
  327.2 14.2 %all-reduce.10.cloned.1.call-done = f32[64,1024]{1,0:T(8,128)} async-done(((f32[64,1024]{1,0:T(8,128)}), f32[64,1024]{1,0:T(8,128)}) %all-reduce.10.cloned.1.call-update) | async-done | bytes 262160 | tf_op jit(solution)/shard_map/psum | solution.py:72
  341.4 1.1 multiply_reduce_fusion
  342.5 42.0 %psum.50 = f32[64]{0:T(128)S(1)} all-reduce(f32[64]{0:T(128)S(1)} %multiply_reduce_fusion), channel_id=1, replica_groups=mesh['tile'=16,'rhs'=2] {'tile'}, use_global_device_ids=true, to_apply=%region_11.12 | all-reduce | flops 64 | bytes 512 | tf_op jit(solution)/shard_map/psum | solution.py:37
  384.5 1.9 multiply_subtract_fusion
  (38 shorter events, 3.8 us)
Async XLA Ops:
  7.2 6.0 %copy-start = (f32[64,1024]{1,0:T(8,128)S(1)}, f32[64,1024]{1,0:T(8,128)}, u32[]{:S(2)}) copy-start(f32[64,1024]{1,0:T(8,128)} %param.7) | copy-start | bytes 786436
  7.2 12.2 %copy-start.1 = (f32[8,128]{1,0:T(8,128)S(1)}, f32[8,128]{1,0:T(8,128)}, u32[]{:S(2)}) copy-start(f32[8,128]{1,0:T(8,128)} %param.6) | copy-start | bytes 12292
  7.2 87.6 %reduce-scatter.7.cloned.1.call-start = ((), (), s32[]{:S(2)}) async-start(), calls=%async_computation.4 | async-start | bytes 1392640
  13.1 143.1 %all-reduce.8.cloned.1.call-start = ((), (), s32[]{:S(2)}) async-start(), calls=%async_computation.2 | async-start | bytes 524288 | tf_op jit(solution)/shard_map/psum | solution.py:72
  13.3 7.0 %collective-permute-start.1 = (f32[64,1,128]{2,1,0:T(1,128)S(1)}, f32[64,1,128]{2,1,0:T(1,128)S(1)}, u32[]{:S(2)}, u32[]{:S(2)}) collective-permute-start(f32[64,1,128]{2,1,0:T(1,128)S(1)} %get-tuple-element.20), channel_id=1, source_target_pairs={{0,2},{2,4},{4,6},{6,8},{8,10},{10,12},{12,14},{14,16},{16,18},{18... | collective-permute-start | bytes 98312 | tf_op jit(solution)/shard_map/ppermute | solution.py:14
  18.1 5.8 %collective-permute-start = (f32[64,1,128]{2,1,0:T(1,128)S(1)}, f32[64,1,128]{2,1,0:T(1,128)S(1)}, u32[]{:S(2)}, u32[]{:S(2)}) collective-permute-start(f32[64,1,128]{2,1,0:T(1,128)S(1)} %get-tuple-element.21), channel_id=1, source_target_pairs={{2,0},{4,2},{6,4},{8,6},{10,8},{12,10},{14,12},{16,14},{18,16},{20... | collective-permute-start | bytes 98312 | tf_op jit(solution)/shard_map/ppermute | solution.py:17
  24.8 116.0 %collective-permute-start.3 = (f32[64,1,128]{2,1,0:T(1,128)S(1)}, f32[64,1,128]{2,1,0:T(1,128)S(1)}, u32[]{:S(2)}, u32[]{:S(2)}) collective-permute-start(f32[64,1,128]{2,1,0:T(1,128)S(1)} %get-tuple-element.18), channel_id=1, source_target_pairs={{0,2},{2,4},{4,6},{6,8},{8,10},{10,12},{12,14},{14,16},{16,18},{18... | collective-permute-start | bytes 98312 | tf_op jit(solution)/shard_map/ppermute | solution.py:14
  29.4 111.4 %collective-permute-start.2 = (f32[64,1,128]{2,1,0:T(1,128)S(1)}, f32[64,1,128]{2,1,0:T(1,128)S(1)}, u32[]{:S(2)}, u32[]{:S(2)}) collective-permute-start(f32[64,1,128]{2,1,0:T(1,128)S(1)} %get-tuple-element.19), channel_id=1, source_target_pairs={{2,0},{4,2},{6,4},{8,6},{10,8},{12,10},{14,12},{16,14},{18,16},{20... | collective-permute-start | bytes 98312 | tf_op jit(solution)/shard_map/ppermute | solution.py:17
  140.8 139.0 %reduce-scatter.9.cloned.1.call-start = ((), (), s32[]{:S(2)}) async-start(), calls=%async_computation.5 | async-start | bytes 1392640
  205.1 136.2 %all-reduce.10.cloned.1.call-start = ((), (), s32[]{:S(2)}) async-start(), calls=%async_computation.3 | async-start | bytes 524288 | tf_op jit(solution)/shard_map/psum | solution.py:72
  205.3 3.1 collective-permute-start.5
  206.6 6.2 %collective-permute-start.4 = (f32[64,1,128]{2,1,0:T(1,128)S(1)}, f32[64,1,128]{2,1,0:T(1,128)S(1)}, u32[]{:S(2)}, u32[]{:S(2)}) collective-permute-start(f32[64,1,128]{2,1,0:T(1,128)S(1)} %get-tuple-element.17), channel_id=1, source_target_pairs={{2,0},{4,2},{6,4},{8,6},{10,8},{12,10},{14,12},{16,14},{18,16},{20... | collective-permute-start | bytes 98312 | tf_op jit(solution)/shard_map/ppermute | solution.py:17
  213.7 112.7 %collective-permute-start.7 = (f32[64,1,128]{2,1,0:T(1,128)S(1)}, f32[64,1,128]{2,1,0:T(1,128)S(1)}, u32[]{:S(2)}, u32[]{:S(2)}) collective-permute-start(f32[64,1,128]{2,1,0:T(1,128)S(1)} %get-tuple-element.14), channel_id=1, source_target_pairs={{0,2},{2,4},{4,6},{6,8},{8,10},{10,12},{12,14},{14,16},{16,18},{18... | collective-permute-start | bytes 98312 | tf_op jit(solution)/shard_map/ppermute | solution.py:14
  216.2 110.1 %collective-permute-start.6 = (f32[64,1,128]{2,1,0:T(1,128)S(1)}, f32[64,1,128]{2,1,0:T(1,128)S(1)}, u32[]{:S(2)}, u32[]{:S(2)}) collective-permute-start(f32[64,1,128]{2,1,0:T(1,128)S(1)} %get-tuple-element.15), channel_id=1, source_target_pairs={{2,0},{4,2},{6,4},{8,6},{10,8},{12,10},{14,12},{16,14},{18,16},{20... | collective-permute-start | bytes 98312 | tf_op jit(solution)/shard_map/ppermute | solution.py:17
Sparse Core Ops, SparseCore 0:
  13.2 81.5 reduce-scatter.6
  140.9 15.2 all-reduce.7
  205.3 74.4 reduce-scatter.8
  326.4 14.9 all-reduce.9
where the time goes:
time: 394 us; the launch traced here: 393 us
  waiting for transfers between devices  164 us (42%)
  blocking collectives  163 us (41%)
  matrix products  21.3 us (5%)
  starting transfers between devices  18.6 us (5%)
  between operations  14.1 us (4%)
  other arithmetic  7.57 us (2%)
  local copies, waits for them, and re-layouts  5.05 us (1%)
    unnamed x6, waiting for transfers between devices  126 us
    psum x2, blocking collectives, joint_products(): lax.psum((jnp.sum(residual * residual, axis=1), jnp.sum(direction * image...  83.9 us
    all_gather x2, blocking collectives, per_device(): lax.all_gather(weighted, 'tile', axis=1, tiled=True)  78.7 us
    psum x2, waiting for transfers between devices, per_device(): image = lax.psum(back_half, 'rhs') + twice.reshape(direction.shape)  28.7 us
    ppermute x4, starting transfers between devices, with_halo(): lax.ppermute(lax.slice_in_dim(block, block.shape[dim] - width, None, axis...  13.3 us
    unnamed x2, matrix products  11.5 us
    dot_general x2, matrix products, per_device(): lax.dot_general(lax.all_gather(weighted, 'tile', axis=1, tiled=True), sen...  9.77 us
    ppermute x4, waiting for transfers between devices, with_halo(): lax.ppermute(lax.slice_in_dim(block, 0, width, axis=dim), axis, backward)  8.1 us
  transfers between devices with their start and end apart: 12, of which 7 were waited for; matrix products, arithmetic and copies ran while one was open for 5% of the time, Pallas kernels for 0%

commit v1 on v0

v1 whole, which is shorter than its diff:
```python
import functools

import jax
import jax.numpy as jnp
from jax import lax
from jax.experimental import pallas as pl
from jax.experimental.pallas import tpu as pltpu
from jax.sharding import PartitionSpec as P

ITERS = 2
LANES = 128
ROWS16 = 16
SPLIT = (3, 2)
F32, BF16 = jnp.float32, jnp.bfloat16


def lane_ids(rows):
    return lax.broadcasted_iota(jnp.int32, (rows, LANES), 1)


def encode(value):
    high = value.astype(BF16).astype(F32)
    lanes = lax.broadcasted_iota(jnp.int32, value.shape, value.ndim - 1)
    return jnp.where(lanes < LANES // 2, high, value - high).astype(BF16)


def decode(piece):
    wide = piece.astype(F32)
    return wide + pltpu.roll(wide, LANES // 2, wide.ndim - 1)


def spread(rows, columns):
    lanes = lane_ids(rows) % (LANES // 2)
    out = jnp.zeros((rows, LANES), F32)
    for lane, column in columns.items():
        out = jnp.where(lanes == lane, column, out)
    return out


def kernel(
    n, chunks, sens_hbm, prec_hbm, reaction_hbm, load_hbm, sol_out, res_out,
    sens, prec, reaction, load, react_in, halo, field1, efield, eetwice,
    pred32, send_a, recv_a, sum_z, send_z, recv_z, pred0, wb, core_send, core_recv, scal,
    esend_a, erecv_a, esend_z, erecv_z, efull,
    load_sem, sems_s, sems_r, halo_s, halo_r, react_s, react_r, core_s, core_r, e_s, e_r,
):
    t = lax.axis_index("tile")
    r = lax.axis_index("rhs")
    rz = n // 4
    x, y, z, g = t % 2, (t // 2) % 2, t // 4, t % 4
    steps_xy = (3 - 2 * x - 4 * y, 1 - 2 * x, 2 - 4 * y)
    count, strip = load.shape
    half = count // 2
    rows = reaction.shape[0]
    obs = sens.shape[1]
    total = sum(chunks) * rz * LANES
    last = len(chunks) - 1
    has_low, has_high = t > 0, t < n - 1

    def to(tile):
        return (tile, r)

    small = []
    for at, (src, dst) in enumerate(((load_hbm, load), (prec_hbm, prec), (reaction_hbm, reaction))):
        copy = pltpu.make_async_copy(src, dst, load_sem.at[len(chunks) + at])
        copy.start()
        small.append(copy)
    starts = [sum(chunks[:c]) for c in range(len(chunks))]
    spans = []
    loads = []
    for c, u in enumerate(chunks):
        lo = min(starts[c] * rz * LANES, obs)
        hi = min((starts[c] + u) * rz * LANES, obs)
        spans.append((lo, hi))
        copy = pltpu.make_async_copy(
            sens_hbm.at[:, lo:hi], sens.at[:, lo:hi], load_sem.at[c]
        )
        copy.start()
        loads.append(copy)

    barrier = pltpu.get_barrier_semaphore()

    def greet(device):
        pl.semaphore_signal(
            barrier, inc=1, device_id=device, device_id_type=pl.DeviceIdType.MESH
        )

    greet((t, 1 - r))
    xy_peers = [t + step for step in steps_xy]
    z_peers = [((z + k) % rz) * 4 + g for k in range(1, rz)]
    for peer in xy_peers + z_peers:
        greet(to(peer))

    @pl.when(has_low)
    def _():
        greet(to(t - 1))

    @pl.when(has_high)
    def _():
        greet(to(t + 1))

    @pl.when(jnp.logical_not(has_low))
    def _():
        for it in range(ITERS):
            halo[it, 0] = jnp.zeros(halo.shape[2:], F32)
        react_in[0] = jnp.zeros(react_in.shape[1:], F32)

    @pl.when(jnp.logical_not(has_high))
    def _():
        for it in range(ITERS):
            halo[it, 1] = jnp.zeros(halo.shape[2:], F32)
        react_in[1] = jnp.zeros(react_in.shape[1:], F32)

    for copy in small:
        copy.wait()
    pl.semaphore_wait(barrier, 3 + rz + (t + n - 1) // n + (2 * n - 2 - t) // n)

    sends = []

    def remote(src, dst, s, q, device):
        return pltpu.make_async_remote_copy(
            src_ref=src, dst_ref=dst, send_sem=s, recv_sem=q,
            device_id=device, device_id_type=pl.DeviceIdType.MESH,
        )

    def launch(*args):
        copy = remote(*args)
        copy.start()
        sends.append(copy)
        return copy

    width = 2 * LANES

    def halo_copies(it, ref):
        down = remote(
            ref.at[:, 0:width], halo.at[it, 1], halo_s.at[it, 0], halo_r.at[it, 1], to(t - 1)
        )
        up = remote(
            ref.at[:, strip - width:strip], halo.at[it, 0],
            halo_s.at[it, 1], halo_r.at[it, 0], to(t + 1),
        )
        return down, up

    def react_copies():
        down = remote(reaction, react_in.at[1], react_s.at[0], react_r.at[1], to(t - 1))
        up = remote(reaction, react_in.at[0], react_s.at[1], react_r.at[0], to(t + 1))
        return down, up

    def start_pair(pair):
        @pl.when(has_low)
        def _():
            pair[0].start()

        @pl.when(has_high)
        def _():
            pair[1].start()

    def arrive_pair(pair):
        @pl.when(has_low)
        def _():
            pair[1].wait_recv()

        @pl.when(has_high)
        def _():
            pair[0].wait_recv()

    def sent_pair(pair):
        @pl.when(has_low)
        def _():
            pair[0].wait_send()

        @pl.when(has_high)
        def _():
            pair[1].wait_send()

    react_pair = react_copies()
    start_pair(react_pair)
    pairs = [halo_copies(0, load), halo_copies(1, field1)]
    start_pair(pairs[0])

    lanes = lane_ids(count)

    def blk(k):
        return slice(k * LANES, (k + 1) * LANES)

    def apply_row(center, above, below, coefficient):
        west = jnp.where(lanes == 0, 0.0, pltpu.roll(center, 1, 1))
        east = jnp.where(lanes == LANES - 1, 0.0, pltpu.roll(center, LANES - 1, 1))
        return (coefficient + 4.0) * center - (above + below + west + east)

    def stencil(it, ref):
        def f(k):
            if k < 0:
                return halo[it, 0][:, blk(k + 2)]
            if k >= rows:
                return halo[it, 1][:, blk(k - rows)]
            return ref[:, blk(k)]

        def coefficient(k):
            if k < 0:
                return react_in[0][rows - 1:rows, :]
            if k >= rows:
                return react_in[1][0:1, :]
            return reaction[k:k + 1, :]

        own = jnp.zeros((count, LANES), F32)
        cross = jnp.zeros((count, LANES), F32)
        for k in range(-1, rows + 1):
            g = apply_row(f(k), f(k - 1), f(k + 1), coefficient(k))
            if k == -1:
                g = jnp.where(has_low, g, 0.0)
            if k == rows:
                g = jnp.where(has_high, g, 0.0)
            efield[it, :, blk(k + 1)] = g
            if 0 <= k < rows:
                own += g * g
                if it:
                    cross += g * efield[0, :, blk(k + 1)]
        for k in range(rows):
            eetwice[it, :, blk(k)] = apply_row(
                efield[it, :, blk(k + 1)], efield[it, :, blk(k)],
                efield[it, :, blk(k + 2)], reaction[k:k + 1, :],
            )
        return jnp.sum(own, axis=1, keepdims=True), jnp.sum(cross, axis=1, keepdims=True)

    def wide_range(c):
        lo = 0 if c == 0 else LANES + starts[c] * rz * LANES
        return lo, LANES + (starts[c] + chunks[c]) * rz * LANES

    def z_range(c):
        lo = 0 if c == 0 else LANES + starts[c] * LANES
        return lo, LANES + (starts[c] + chunks[c]) * LANES

    def out_range(c):
        lo = starts[c] * rz * LANES
        hi = lo + chunks[c] * rz * LANES + (rz * LANES if c == last else 0)
        return lo, hi

    def iteration(it, ref):
        sem = lambda c, k: (sems_s.at[it, c, k], sems_r.at[it, c, k])
        esem = lambda k: (e_s.at[it, k], e_r.at[it, k])
        inflight = {}
        state = {}

        def put_wide(lo, hi, value):
            shaped = value.reshape(4, ROWS16, hi - lo)
            pred32[:, :, lo:hi] = shaped
            return shaped

        def product(c):
            if it == 0:
                loads[c].wait()
            lo = LANES + starts[c] * rz * LANES
            hi = lo + chunks[c] * rz * LANES
            s_lo, s_hi = spans[c]
            mid = lo + s_hi - s_lo
            if mid > lo:
                part = jnp.dot(
                    state["lowered"], sens[:, s_lo:s_hi], preferred_element_type=F32
                )
                send_a[it, :, :, lo:mid] = put_wide(lo, mid, part).astype(BF16)
            if mid < hi:
                rest = put_wide(mid, hi, jnp.zeros((count, hi - mid), F32))
                send_a[it, :, :, mid:hi] = rest.astype(BF16)
            if c == 0:
                whole = ref[...]
                square = jnp.sum(whole * whole, axis=1, keepdims=True)
                send_a[it, :, :, 0:LANES] = encode(put_wide(0, LANES, spread(count, {0: square})))
            lo, hi = wide_range(c)
            for k in range(3):
                inflight["a", c, k] = launch(
                    send_a.at[it, g + steps_xy[k], :, lo:hi], recv_a.at[it, k, :, lo:hi],
                    *sem(c, k), to(xy_peers[k]),
                )

        def sum_xy(c):
            for k in range(3):
                inflight["a", c, k].wait_recv()
            lo = LANES + starts[c] * rz * LANES
            u = chunks[c] * LANES
            hi = lo + rz * u
            value = pred32[g, :, lo:hi]
            for k in (1, 2, 0):
                value += recv_a[it, k, :, lo:hi].astype(F32)
            sum_z[:, lo:hi] = value
            z_lo, z_hi = z_range(c)
            for j in range(rz):
                send_z[it, j, :, z_hi - u:z_hi] = value[:, j * u:(j + 1) * u]
            if c == 0:
                value = pred32[g, :, 0:LANES]
                for k in (1, 2, 0):
                    value += decode(recv_a[it, k, :, 0:LANES])
                sum_z[:, 0:LANES] = value
                for j in range(rz):
                    send_z[it, j, :, 0:LANES] = value
            for k in range(1, rz):
                inflight["z", c, k] = launch(
                    send_z.at[it, (z + k) % rz, :, z_lo:z_hi], recv_z.at[it, k - 1, :, z_lo:z_hi],
                    *sem(c, 2 + k), to(z_peers[k - 1]),
                )

        def smooth_part():
            if it:
                start_pair(pairs[it])

        def smooth_xy():
            arrive_pair(pairs[it])
            if it == 0:
                arrive_pair(react_pair)
            own, cross = stencil(it, ref)
            value = spread(count, {1: own, 3: cross})
            efull[...] = value
            state["e"] = efull[pl.ds(pl.multiple_of(r * half, half), half), :]
            esend_a[it] = encode(state["e"])
            for k in range(3):
                inflight["ea", k] = launch(
                    esend_a.at[it], erecv_a.at[it, k], *esem(k), to(xy_peers[k])
                )

        def smooth_z():
            for k in range(3):
                inflight["ea", k].wait_recv()
            for k in (1, 2, 0):
                state["e"] += decode(erecv_a[it, k])
            esend_z[it] = encode(state["e"])
            for k in range(1, rz):
                inflight["ez", k] = launch(
                    esend_z.at[it], erecv_z.at[it, k - 1], *esem(2 + k), to(z_peers[k - 1])
                )

        def smooth_all():
            for k in range(1, rz):
                inflight["ez", k].wait_recv()
                state["e"] += decode(erecv_z[it, k - 1])

        def weigh(c):
            for k in range(1, rz):
                inflight["z", c, k].wait_recv()
            u = chunks[c] * LANES
            z_hi = z_range(c)[1]
            z_lo = z_hi - u
            column = pl.multiple_of(starts[c] * rz * LANES + z * u, LANES)
            own = sum_z[:, pl.ds(pl.multiple_of(LANES + column, LANES), u)]
            for k in range(1, rz):
                own += recv_z[it, k - 1, :, z_lo:z_hi]
            if c == 0:
                fresh = sum_z[:, 0:LANES]
                for k in range(1, rz):
                    fresh += recv_z[it, k - 1, :, 0:LANES]
                state["fresh"] = fresh[:, 0:1]
                if it:
                    state["beta"] = state["fresh"] / scal[g, :, 0:1]
            if it == 0:
                pred0[:, starts[c] * LANES:starts[c] * LANES + u] = own
            else:
                own += state["beta"] * pred0[:, starts[c] * LANES:starts[c] * LANES + u]
            scaled = prec[:, pl.ds(column, u)] * own
            wb[it, g, :, pl.ds(column, u)] = scaled.astype(BF16)
            ref_own = wb.at[it, g, :, pl.ds(column, u)]
            for k in range(1, rz):
                inflight["gz", c, k] = launch(
                    ref_own, ref_own, *sem(c, rz + 1 + k), to(z_peers[k - 1])
                )
            curved = jnp.sum(scaled * own, axis=1, keepdims=True)
            state["curved"] = curved if c == 0 else state["curved"] + curved
            if c == last:
                place = pl.multiple_of(total + z * LANES, LANES)
                wb[it, g, :, pl.ds(place, LANES)] = encode(spread(
                    ROWS16, {0: state["fresh"] * (1.0 / (2 * rz)), 2: state["curved"]},
                ))
                ref_own = wb.at[it, g, :, pl.ds(place, LANES)]
                for k in range(1, rz):
                    inflight["gs", k] = launch(
                        ref_own, ref_own, *sem(c, 2 * rz + k), to(z_peers[k - 1])
                    )

        def hand_on(c):
            for k in range(1, rz):
                inflight["gz", c, k].wait_recv()
                if c == last:
                    inflight["gs", k].wait_recv()
            lo, hi = out_range(c)
            piece = wb.at[it, g, :, lo:hi]
            for k in range(3):
                inflight["g", c, k] = launch(piece, piece, *sem(c, 3 * rz + k), to(xy_peers[k]))

        def back(c):
            for k in range(3):
                inflight["g", c, k].wait_recv()
            lo, hi = spans[c]
            if hi > lo:
                left = wb[it, :, :, lo:hi].reshape(count, hi - lo)
                part = lax.dot_general(
                    left, sens[:, lo:hi], (((1,), (1,)), ((), ())), preferred_element_type=F32
                )
                if c == 0:
                    core_send[it, :, 0:strip] = part
                else:
                    core_send[it, :, 0:strip] += part

        def meet():
            sums = jnp.zeros((count, LANES), F32)
            for j in range(rz):
                piece = wb[it, :, :, total + j * LANES:total + (j + 1) * LANES]
                sums += decode(piece.reshape(count, LANES))
            core_send[it, :, strip:strip + LANES] = sums
            core_send[it, pl.ds(pl.multiple_of(r * half, half), half), strip:strip + LANES] += state["e"]
            copy = launch(
                core_send.at[it], core_recv.at[it], core_s.at[it], core_r.at[it], (t, 1 - r)
            )
            copy.wait_recv()

        state["lowered"] = ref[...].astype(BF16)
        each = range(len(chunks))
        for c in each:
            product(c)
        smooth_part()
        for c in each:
            sum_xy(c)
        smooth_xy()
        for c in each:
            weigh(c)
        smooth_z()
        for c in each:
            hand_on(c)
        smooth_all()
        for c in each:
            back(c)
        meet()
        sums = core_send[it, :, strip:strip + LANES] + core_recv[it, :, strip:strip + LANES]
        scal[...] = sums.reshape(4, ROWS16, LANES)
        return sums

    def back_of(it, k):
        return core_send[it, :, blk(k)] + core_recv[it, :, blk(k)]

    sums0 = iteration(0, load)
    alpha0 = sums0[:, 0:1] / (sums0[:, 1:2] + sums0[:, 2:3])
    for k in range(rows):
        field1[:, blk(k)] = load[:, blk(k)] - alpha0 * (back_of(0, k) + eetwice[0, :, blk(k)])
    sums1 = iteration(1, field1)
    beta = sums1[:, 0:1] / sums0[:, 0:1]
    smooth = sums1[:, 1:2] + 2.0 * beta * sums1[:, 3:4] + beta * beta * sums0[:, 1:2]
    alpha1 = sums1[:, 0:1] / (smooth + sums1[:, 2:3])
    for k in range(rows):
        first, second = load[:, blk(k)], field1[:, blk(k)]
        image = back_of(1, k) + (eetwice[1, :, blk(k)] + beta * eetwice[0, :, blk(k)])
        sol_out[:, blk(k)] = alpha0 * first + alpha1 * (second + beta * first)
        res_out[:, blk(k)] = second - alpha1 * image
    for copy in sends:
        copy.wait_send()
    for pair in [react_pair] + pairs:
        sent_pair(pair)


def per_device(n, sensitivity, precision, reaction, load):
    count, strip = load.shape
    rows = reaction.shape[0]
    obs = sensitivity.shape[1]
    rz = n // 4
    units = -(-obs // (rz * LANES))
    chunks = SPLIT if sum(SPLIT) == units else (units,)
    total = units * rz * LANES
    padded = jnp.pad(precision, (0, total - obs)).reshape(1, total)
    wide, narrow = total + LANES, (units + 1) * LANES
    slots = 3 * rz + 3
    vm = pltpu.VMEM
    dma = pltpu.SemaphoreType.DMA
    out = jax.ShapeDtypeStruct(load.shape, F32)
    return pl.pallas_call(
        functools.partial(kernel, n, chunks),
        out_shape=(out, out),
        in_specs=[pl.BlockSpec(memory_space=pl.ANY)] * 4,
        out_specs=(pl.BlockSpec(memory_space=vm),) * 2,
        scratch_shapes=[
            vm(sensitivity.shape, BF16),
            vm(padded.shape, F32),
            vm(reaction.shape, F32),
            vm(load.shape, F32),
            vm((2, rows, LANES), F32),
            vm((ITERS, 2, count, 2 * LANES), F32),
            vm((count, strip), F32),
            vm((ITERS, count, strip + 2 * LANES), F32),
            vm((ITERS, count, strip), F32),
            vm((4, ROWS16, wide), F32),
            vm((ITERS, 4, ROWS16, wide), BF16),
            vm((ITERS, 3, ROWS16, wide), BF16),
            vm((ROWS16, wide), F32),
            vm((ITERS, rz, ROWS16, narrow), F32),
            vm((ITERS, rz - 1, ROWS16, narrow), F32),
            vm((ROWS16, units * LANES), F32),
            vm((ITERS, 4, ROWS16, total + rz * LANES), BF16),
            vm((ITERS, count, strip + LANES), F32),
            vm((ITERS, count, strip + LANES), F32),
            vm((4, ROWS16, LANES), F32),
            vm((ITERS, count // 2, LANES), BF16),
            vm((ITERS, 3, count // 2, LANES), BF16),
            vm((ITERS, count // 2, LANES), BF16),
            vm((ITERS, rz - 1, count // 2, LANES), BF16),
            vm((count, LANES), F32),
            dma((len(chunks) + 3,)),
            dma((ITERS, len(chunks), slots)),
            dma((ITERS, len(chunks), slots)),
            dma((ITERS, 2)),
            dma((ITERS, 2)),
            dma((2,)),
            dma((2,)),
            dma((ITERS,)),
            dma((ITERS,)),
            dma((ITERS, 2 + rz)),
            dma((ITERS, 2 + rz)),
        ],
        compiler_params=pltpu.CompilerParams(
            collective_id=0, has_side_effects=True, vmem_limit_bytes=48 * 2**20
        ),
    )(sensitivity, padded, reaction, load)


def solution(mesh):
    placed = (P("tile", "rhs"), P("rhs"), P("tile", None), P(None, "tile"))
    return jax.shard_map(
        functools.partial(per_device, mesh.shape["tile"]),
        mesh=mesh,
        in_specs=placed,
        out_specs=(P(None, "tile"), P(None, "tile")),
        check_vma=False,
    )
```

time: 394 us -> 60.7 us (0.15)
  waiting for transfers between devices: 164 us -> 0 us
  blocking collectives: 163 us -> 0 us
  Pallas kernels: 0 us -> 53.2 us
  matrix products: 21.3 us -> 0 us
  starting transfers between devices: 18.6 us -> 0 us
  between operations: 14.1 us -> 0.64 us
  other arithmetic: 7.57 us -> 0 us
    unnamed x6 -> x0, waiting for transfers between devices: 126 us -> none
    psum x2 -> x0, blocking collectives: 83.9 us -> none  [joint_products(): lax.psum((jnp.sum(residual * residual, axis=1), jnp.sum(direction * image...]
    all_gather x2 -> x0, blocking collectives: 78.7 us -> none  [per_device(): lax.all_gather(weighted, 'tile', axis=1, tiled=True)]
    pallas_call x0 -> x1, Pallas kernels: none -> 53.2 us  [per_device(): pl.pallas_call(functools.partial(kernel, n, chunks), out_shape=(out, out)...]
    psum x2 -> x0, waiting for transfers between devices: 28.7 us -> none  [per_device(): image = lax.psum(back_half, 'rhs') + twice.reshape(direction.shape)]
    ppermute x8 -> x0, starting transfers between devices: 18.4 us -> none  [the longest x4 13.3 us: with_halo(): lax.ppermute(lax.slice_in_dim(block, block.shape[dim] - width, None, axis...]
    unnamed x2 -> x0, matrix products: 11.5 us -> none
    dot_general x2 -> x0, matrix products: 9.77 us -> none  [per_device(): lax.dot_general(lax.all_gather(weighted, 'tile', axis=1, tiled=True), sen...]
  transfers between devices with their start and end apart: 12 -> 0, of which waited for: 7 -> 0; matrix products, arithmetic and copies ran while one was open for 5% -> 0% of each run, Pallas kernels for 0% -> 0%
where the time goes in v1:
time: 60.7 us; the launch traced here: 60.1 us
  Pallas kernels  53.2 us (88%)
  local copies, waits for them, and re-layouts  6.24 us (10%)
  between operations  0.64 us (1%)
    pallas_call x1, Pallas kernels, per_device(): pl.pallas_call(functools.partial(kernel, n, chunks), out_shape=(out, out)...  53.2 us
    unnamed x8, local copies, waits for them, and re-layouts  5.53 us

profile of v1, /device:TPU:0, one launch (start us, length us, event | category | flops | bytes accessed | tf_op | source)
XLA Modules:
  0.0 60.1 jit_solution(17282907233378866061)
XLA Ops:
  0.6 0.7 %reshape.7.prec_hbm = f32[1,2560]{1,0:T(1,128)S(1)} reshape(f32[2560]{0:T(1024)} %param.5) | data formatting | bytes 20480 | tf_op jit(solution)/shard_map/reshape | solution.py:464
  1.3 0.0 copy-start
  1.3 2.5 %copy-done = bf16[1024,2560]{1,0:T(8,128)(2,1)S(1)} copy-done((bf16[1024,2560]{1,0:T(8,128)(2,1)S(1)}, bf16[1024,2560]{1,0:T(8,128)(2,1)}, u32[]{:S(2)}) %copy-start) | copy-done | bytes 5242904
  3.8 0.0 copy-start.1
  3.8 0.9 %copy-done.1 = f32[64,1024]{1,0:T(8,128)S(1)} copy-done((f32[64,1024]{1,0:T(8,128)S(1)}, f32[64,1024]{1,0:T(8,128)}, u32[]{:S(2)}) %copy-start.1) | copy-done | bytes 262168
  4.8 0.0 copy-start.2
  4.8 0.7 %copy-done.2 = f32[8,128]{1,0:T(8,128)S(1)} copy-done((f32[8,128]{1,0:T(8,128)S(1)}, f32[8,128]{1,0:T(8,128)}, u32[]{:S(2)}) %copy-start.2) | copy-done | bytes 4120
  5.5 53.2 %shard_map.59 = (f32[64,1024]{1,0:T(8,128)S(1)}, f32[64,1024]{1,0:T(8,128)S(1)}) custom-call(bf16[1024,2560]{1,0:T(8,128)(2,1)S(1)} %copy-done, f32[1,2560]{1,0:T(1,128)S(1)} %reshape.7.prec_hbm, f32[8,128]{1,0:T(8,128)S(1)} %copy-done.2, f32[64,1024]{1,0:T(8,128)S(1)} %copy-done.1), custom_call_target="tpu_custom_call" | custom-call | tf_op jit(solution)/shard_map/pallas_call | solution.py:470
  58.7 0.7 %copy.8 = f32[64,1024]{1,0:T(8,128)} copy(f32[64,1024]{1,0:T(8,128)S(1)} %get-tuple-element.4) | data formatting | bytes 524288
  59.4 0.7 %copy.9 = f32[64,1024]{1,0:T(8,128)} copy(f32[64,1024]{1,0:T(8,128)S(1)} %get-tuple-element.5) | data formatting | bytes 524288
Async XLA Ops:
  1.3 2.5 %copy-start = (bf16[1024,2560]{1,0:T(8,128)(2,1)S(1)}, bf16[1024,2560]{1,0:T(8,128)(2,1)}, u32[]{:S(2)}) copy-start(bf16[1024,2560]{1,0:T(8,128)(2,1)} %sens_hbm.1) | copy-start | bytes 15728644
  3.8 0.9 %copy-start.1 = (f32[64,1024]{1,0:T(8,128)S(1)}, f32[64,1024]{1,0:T(8,128)}, u32[]{:S(2)}) copy-start(f32[64,1024]{1,0:T(8,128)} %load_hbm.1) | copy-start | bytes 786436
  4.8 0.7 %copy-start.2 = (f32[8,128]{1,0:T(8,128)S(1)}, f32[8,128]{1,0:T(8,128)}, u32[]{:S(2)}) copy-start(f32[8,128]{1,0:T(8,128)} %reaction_hbm.1) | copy-start | bytes 12292

commit v2 on v1

--- a/solution.py
+++ b/solution.py
@@ -10,7 +10,7 @@
 ITERS = 2
 LANES = 128
 ROWS16 = 16
-SPLIT = (3, 2)
+SPLIT = (1, 2, 2)
 F32, BF16 = jnp.float32, jnp.bfloat16
 
 

time: 60.7 us -> 58.6 us (0.965)
  Pallas kernels: 53.2 us -> 51.1 us
    pallas_call x1, Pallas kernels: 53.2 us -> 51.1 us  [per_device(): pl.pallas_call(functools.partial(kernel, n, chunks), out_shape=(out, out)...]
where the time goes in v2:
time: 58.6 us; the launch traced here: 58 us
  Pallas kernels  51.1 us (87%)
  local copies, waits for them, and re-layouts  6.24 us (11%)
  between operations  0.64 us (1%)
    pallas_call x1, Pallas kernels, per_device(): pl.pallas_call(functools.partial(kernel, n, chunks), out_shape=(out, out)...  51.1 us
    unnamed x8, local copies, waits for them, and re-layouts  5.53 us

profile of v2, /device:TPU:0, one launch (start us, length us, event | category | flops | bytes accessed | tf_op | source)
XLA Modules:
  0.0 58.0 jit_solution(6273761836466275310)
XLA Ops:
  0.6 0.7 %reshape.7.prec_hbm = f32[1,2560]{1,0:T(1,128)S(1)} reshape(f32[2560]{0:T(1024)} %param.5) | data formatting | bytes 20480 | tf_op jit(solution)/shard_map/reshape | solution.py:464
  1.3 0.0 copy-start
  1.3 2.5 %copy-done = bf16[1024,2560]{1,0:T(8,128)(2,1)S(1)} copy-done((bf16[1024,2560]{1,0:T(8,128)(2,1)S(1)}, bf16[1024,2560]{1,0:T(8,128)(2,1)}, u32[]{:S(2)}) %copy-start) | copy-done | bytes 5242904
  3.8 0.0 copy-start.1
  3.8 0.9 %copy-done.1 = f32[64,1024]{1,0:T(8,128)S(1)} copy-done((f32[64,1024]{1,0:T(8,128)S(1)}, f32[64,1024]{1,0:T(8,128)}, u32[]{:S(2)}) %copy-start.1) | copy-done | bytes 262168
  4.8 0.0 copy-start.2
  4.8 0.7 %copy-done.2 = f32[8,128]{1,0:T(8,128)S(1)} copy-done((f32[8,128]{1,0:T(8,128)S(1)}, f32[8,128]{1,0:T(8,128)}, u32[]{:S(2)}) %copy-start.2) | copy-done | bytes 4120
  5.5 51.1 %shard_map.59 = (f32[64,1024]{1,0:T(8,128)S(1)}, f32[64,1024]{1,0:T(8,128)S(1)}) custom-call(bf16[1024,2560]{1,0:T(8,128)(2,1)S(1)} %copy-done, f32[1,2560]{1,0:T(1,128)S(1)} %reshape.7.prec_hbm, f32[8,128]{1,0:T(8,128)S(1)} %copy-done.2, f32[64,1024]{1,0:T(8,128)S(1)} %copy-done.1), custom_call_target="tpu_custom_call" | custom-call | tf_op jit(solution)/shard_map/pallas_call | solution.py:470
  56.6 0.7 %copy.8 = f32[64,1024]{1,0:T(8,128)} copy(f32[64,1024]{1,0:T(8,128)S(1)} %get-tuple-element.4) | data formatting | bytes 524288
  57.3 0.7 %copy.9 = f32[64,1024]{1,0:T(8,128)} copy(f32[64,1024]{1,0:T(8,128)S(1)} %get-tuple-element.5) | data formatting | bytes 524288
Async XLA Ops:
  1.3 2.5 %copy-start = (bf16[1024,2560]{1,0:T(8,128)(2,1)S(1)}, bf16[1024,2560]{1,0:T(8,128)(2,1)}, u32[]{:S(2)}) copy-start(bf16[1024,2560]{1,0:T(8,128)(2,1)} %sens_hbm.1) | copy-start | bytes 15728644
  3.8 0.9 %copy-start.1 = (f32[64,1024]{1,0:T(8,128)S(1)}, f32[64,1024]{1,0:T(8,128)}, u32[]{:S(2)}) copy-start(f32[64,1024]{1,0:T(8,128)} %load_hbm.1) | copy-start | bytes 786436
  4.8 0.7 %copy-start.2 = (f32[8,128]{1,0:T(8,128)S(1)}, f32[8,128]{1,0:T(8,128)}, u32[]{:S(2)}) copy-start(f32[8,128]{1,0:T(8,128)} %reaction_hbm.1) | copy-start | bytes 12292
